TPU v7x, 256 devices: a whole 4x4x8 slice. The times are simulated.
256 devices in a mesh: ctx: 32 (over y, z), tp: 8 (over x, core).
Axes of the slice: x: 4, y: 4, z: 8, core: 2. Of those that a mesh axis runs over, the one named last changes fastest.
Arguments:
- context_block_rows: bfloat16 [16384, 8192], P('ctx', 'tp'), may hold values from -16 to 16
- query_hidden_rows: bfloat16 [64, 8192], P(None, 'tp'), may hold values from -16 to 16
- query_token_positions: int32 [64], replicated, may hold values from 16384 to 16573, as said below
- query_bound: int32 [64], replicated, may hold values from 1 to 16384, as said below
- query_matrix: bfloat16 [8192, 8192], P('ctx', 'tp'), may hold values from -0.0625 to 0.0625
- key_matrix: bfloat16 [8192, 1024], P('ctx', 'tp'), may hold values from -0.0625 to 0.0625
- value_matrix: bfloat16 [8192, 1024], P('ctx', 'tp'), may hold values from -0.0625 to 0.0625
Outputs:
- block_out: bfloat16 [16384, 8192], P('ctx', 'tp')
- query_out: bfloat16 [64, 8192], P(None, 'tp')
Inputs may be any that keep to these rules, and one draw needn't show every extreme that they name: query_token_positions rise strictly with the index; the first is 16384 and the last 16573. `query_bound`: some query token sees all 16384 context tokens.
All inputs are finite; a program needn't handle non-finite values.
Results may differ from a plain program's by a relative error of at most 0.0059.
The roundings to bfloat16 on the way count: a program that leaves them out, or rounds other values in their place, can miss the bound.
Values may be sent and summed in bfloat16 or wider, within the bound.
A program may use at most 128 MiB of HBM per device.

v0:
```python
import math
import jax
import jax.numpy as jnp
from jax import lax
from jax.sharding import PartitionSpec as P

HEAD_SIZE = 128


def from_root(value, axis, source):
    kept = jnp.where(lax.axis_index(axis) == source, value, 0).astype(value.dtype)
    return lax.psum(kept, axis)


def rope_table(half):
    values = []
    for index in range(half):
        freq = 500000.0 ** (-2.0 * index / (2.0 * half))
        wavelen = 2.0 * math.pi / freq
        if wavelen > 8192.0:
            values.append(freq / 8.0)
        elif wavelen < 2048.0:
            values.append(freq)
        else:
            smooth = (8192.0 / wavelen - 1.0) / 3.0
            values.append((1.0 - smooth) * freq / 8.0 + smooth * freq)
    return values


def apply_rotary(values, token_positions):
    half = values.shape[-1] // 2
    freqs = jnp.asarray(rope_table(half), jnp.float32)
    angle = token_positions.astype(jnp.float32)[:, None] * freqs[None, :]
    cosine = jnp.cos(angle)[:, None, :]
    sine = jnp.sin(angle)[:, None, :]
    first = values[..., :half]
    second = values[..., half:]
    return jnp.concatenate([first * cosine - second * sine, second * cosine + first * sine], -1)


def attend(query_heads_split, keys, values, valid):
    scale = 1.0 / math.sqrt(query_heads_split.shape[-1])
    scores = (
        jnp.einsum("qkgd,skd->qkgs", query_heads_split, keys, preferred_element_type=jnp.float32)
        * scale
    )
    scores = jnp.where(valid[:, None, None, :], scores, -1e30)
    peak = jnp.max(scores, -1)
    weights = jnp.exp(scores - peak[..., None])
    total = jnp.sum(weights, -1)
    mixed = jnp.einsum(
        "qkgs,skd->qkgd", weights.astype(jnp.bfloat16), values, preferred_element_type=jnp.float32
    )
    return (peak, total, mixed)


def on_device(
    context_block_rows,
    query_hidden_rows,
    query_token_positions,
    query_bound,
    query_matrix,
    key_matrix,
    value_matrix,
):
    ctx_index = lax.axis_index("ctx")
    blk = context_block_rows.shape[0]
    qcount = query_hidden_rows.shape[0]
    heads_q = query_matrix.shape[1] // HEAD_SIZE
    heads_kv = key_matrix.shape[1] // HEAD_SIZE
    head_group = heads_q // heads_kv
    whole_rows, whole_query = (
        lax.all_gather(context_block_rows, "tp", axis=1, tiled=True),
        lax.all_gather(query_hidden_rows, "tp", axis=1, tiled=True),
    )
    stacked = jnp.concatenate([whole_rows, whole_query], 0)
    head_rows = blk + qcount
    proj_query = jnp.dot(
        stacked,
        lax.all_gather(query_matrix, "ctx", axis=0, tiled=True),
        preferred_element_type=jnp.float32,
    )
    proj_key = jnp.dot(
        stacked,
        lax.all_gather(key_matrix, "ctx", axis=0, tiled=True),
        preferred_element_type=jnp.float32,
    )
    proj_value = jnp.dot(
        stacked,
        lax.all_gather(value_matrix, "ctx", axis=0, tiled=True),
        preferred_element_type=jnp.float32,
    )
    local_pos = ctx_index * blk + jnp.arange(blk, dtype=jnp.int32)
    k_block = apply_rotary(proj_key[:blk].reshape(blk, heads_kv, HEAD_SIZE), local_pos).astype(
        jnp.bfloat16
    )
    v_block = proj_value[:blk].reshape(blk, heads_kv, HEAD_SIZE).astype(jnp.bfloat16)
    key_token_rows = apply_rotary(
        proj_key[blk:head_rows].reshape(qcount, heads_kv, HEAD_SIZE), query_token_positions
    ).astype(jnp.bfloat16)
    value_token_rows = (
        proj_value[blk:head_rows].reshape(qcount, heads_kv, HEAD_SIZE).astype(jnp.bfloat16)
    )
    anchor_key, anchor_value = (from_root(k_block, "ctx", 0), from_root(v_block, "ctx", 0))
    q_block = apply_rotary(proj_query[:blk].reshape(blk, heads_q, HEAD_SIZE), local_pos).astype(
        jnp.bfloat16
    )
    query_token_rows = (
        apply_rotary(proj_query[blk:].reshape(qcount, heads_q, HEAD_SIZE), query_token_positions)
        .astype(jnp.bfloat16)
        .reshape(qcount, heads_kv, head_group, HEAD_SIZE)
    )
    keys_cat = jnp.concatenate([anchor_key, k_block], 0)
    values_cat = jnp.concatenate([anchor_value, v_block], 0)
    anchor_live = ctx_index > 0
    rows_step = min(blk, 512)
    rows_here = 0 + jnp.arange(rows_step, dtype=jnp.int32)
    valid = jnp.concatenate(
        [
            jnp.broadcast_to(anchor_live, (rows_step, blk)),
            rows_here[:, None] >= jnp.arange(blk, dtype=jnp.int32)[None, :],
        ],
        1,
    )
    query_heads_split = q_block.reshape(rows_step, heads_kv, head_group, HEAD_SIZE)
    peak, total, mixed = attend(query_heads_split, keys_cat, values_cat, valid)
    outputs = (
        (mixed / total[..., None]).astype(jnp.bfloat16).reshape(rows_step, heads_q * HEAD_SIZE)
    )
    valid_ctx = local_pos[None, :] < query_bound[:, None]
    peak, total, mixed = attend(query_token_rows, k_block, v_block, valid_ctx)
    top = lax.pmax(peak, "ctx")
    scaled = jnp.exp(peak - top)
    total_all, mixed_all = lax.psum((total * scaled, mixed * scaled[..., None]), "ctx")
    own = jnp.arange(qcount, dtype=jnp.int32)
    self_peak, self_total, self_mixed = attend(
        query_token_rows, key_token_rows, value_token_rows, own[:, None] >= own[None, :]
    )
    final = jnp.maximum(top, self_peak)
    w_ctx = jnp.exp(top - final)
    w_self = jnp.exp(self_peak - final)
    query_out = (mixed_all * w_ctx[..., None] + self_mixed * w_self[..., None]) / (
        total_all * w_ctx + self_total * w_self
    )[..., None]
    query_out = query_out.astype(jnp.bfloat16).reshape(qcount, heads_q * HEAD_SIZE)
    return (outputs, query_out)


def solution(mesh):
    placed = (
        P("ctx", "tp"),
        P(None, "tp"),
        P(),
        P(),
        P("ctx", "tp"),
        P("ctx", "tp"),
        P("ctx", "tp"),
    )
    return jax.shard_map(
        on_device,
        mesh=mesh,
        in_specs=placed,
        out_specs=(P("ctx", "tp"), P(None, "tp")),
        check_vma=False,
    )
```

profile of v0, /device:TPU:2, one launch (start us, length us, event | category | flops | bytes accessed | tf_op | source)
XLA Modules:
  0.0 689.7 jit_solution(3943614140132584248)
XLA Ops:
  12.3 1.4 broadcast_compare_fusion
  14.5 2.5 multiply_cosine_fusion
  17.0 47.3 %all-gather.6.cloned.1.call-done = bf16[512,8192]{1,0:T(8,128)(2,1)} async-done(((bf16[512,1024]{1,0:T(8,128)(2,1)}), bf16[512,8192]{1,0:T(8,128)(2,1)}) %all-gather.6.cloned.1.call-update) | async-done | bytes 8388624 | tf_op jit(solution)/shard_map/all_gather | solution.py:73
  64.3 7.6 %constant_dynamic-update-slice_fusion.1 = bf16[576,8192]{1,0:T(8,128)(2,1)} fusion(bf16[512,8192]{1,0:T(8,128)(2,1)} %all-gather.6.cloned.1.call-done), kind=kLoop, calls=%fused_computation.100 | loop fusion | bytes 16777216
  71.9 19.5 %all-gather.8.cloned.1.call-done = bf16[64,8192]{1,0:T(8,128)(2,1)} async-done(((bf16[64,1024]{1,0:T(8,128)(2,1)}), bf16[64,8192]{1,0:T(8,128)(2,1)}) %all-gather.8.cloned.1.call-update) | async-done | bytes 1048592 | tf_op jit(solution)/shard_map/all_gather | solution.py:74
  91.4 2.3 constant_dynamic-update-slice_fusion
  93.7 79.8 %all-gather.12.cloned.1.call-done = bf16[8192,128]{1,0:T(8,128)(2,1)} async-done(((bf16[256,128]{1,0:T(8,128)(2,1)}), bf16[8192,128]{1,0:T(8,128)(2,1)}) %all-gather.12.cloned.1.call-update) | async-done | bytes 2097168 | tf_op jit(solution)/shard_map/all_gather | solution.py:85
  173.5 5.8 fusion.83
  182.2 68.9 %all-gather.10.cloned.1.call-done = bf16[8192,128]{1,0:T(8,128)(2,1)} async-done(((bf16[256,128]{1,0:T(8,128)(2,1)}), bf16[8192,128]{1,0:T(8,128)(2,1)}) %all-gather.10.cloned.1.call-update) | async-done | bytes 2097168 | tf_op jit(solution)/shard_map/all_gather | solution.py:90
  251.1 6.9 convolution_convert_fusion
  258.9 132.5 %all-gather.14.cloned.1.call-done = bf16[8192,1024]{1,0:T(8,128)(2,1)} async-done(((bf16[256,1024]{1,0:T(8,128)(2,1)}), bf16[8192,1024]{1,0:T(8,128)(2,1)}) %all-gather.14.cloned.1.call-update) | async-done | bytes 16777232 | tf_op jit(solution)/shard_map/all_gather | solution.py:80
  391.4 14.9 %fusion.84 = f32[576,1024]{1,0:T(8,128)S(1)} fusion(bf16[576,8192]{1,0:T(8,128)(2,1)} %constant_dynamic-update-slice_fusion, bf16[8192,1024]{1,0:T(8,128)(2,1)} %all-gather.14.cloned.1.call-done), kind=kOutput, calls=%fused_computation.126 | convolution fusion | flops 9663676416 | bytes 28573696 | tf_op jit(solution)/shard_map/dot_general | solution.py:78
  406.8 1.4 fusion.81
  409.1 71.4 %pmax.7 = f32[64,1,8]{0,2,1:T(8,128)S(1)} all-reduce(f32[64,1,8]{0,2,1:T(8,128)S(1)} %bitcast.169), channel_id=1, replica_groups=mesh['ctx'=32,'tp'=8] {'ctx'}, use_global_device_ids=true, to_apply=%region_5.6 | all-reduce | flops 512 | bytes 4096 | tf_op jit(solution)/shard_map/pmax | solution.py:132
  481.1 2.0 fusion.79
  484.8 3.5 subtract_convert_fusion
  488.2 47.8 %all-reduce.7.cloned.1.call-done = (bf16[512,1,128]{2,0,1:T(8,128)(2,1)}, bf16[512,1,128]{2,0,1:T(8,128)(2,1)}) async-done(((bf16[512,1,128]{2,0,1:T(8,128)(2,1)}, bf16[512,1,128]{2,0,1:T(8,128)(2,1)}), (bf16[512,1,128]{2,0,1:T(8,128)(2,1)}, bf16[512,1,128]{2,0,1:T(8,128)(2,1)})) %all-reduce.7.cloned.1.call-update) | async-done | bytes 262160 | tf_op jit(solution)/shard_map/psum | solution.py:12
  536.1 10.7 %fusion.2 = (f32[512,8]{0,1:T(8,128)S(1)}, f32[1024,512,8]{1,0,2:T(8,128)}) fusion(pred[512,1024]{0,1:T(8,128)(4,1)} %concatenate.62, bf16[512,8,64]{2,0,1:T(8,128)(2,1)} %get-tuple-element.9, bf16[512,8,64]{2,0,1:T(8,128)(2,1)S(1)} %get-tuple-element.8, bf16[512,1,64]{2,0,1:T(8,128)(2,1)} %copy-done.1, bf16[512,1,64]{2,0,1:T(8,128)(2,1)S(1)} %get-tuple-element.14, ...), kind=kOutput, calls=%fused_computation.4 | convolution fusion | flops 1089204224 | bytes 18628608 | tf_op jit(solution)/shard_map/qkgd,skd->qkgs/dot_general | solution.py:44
  546.8 9.3 %fusion = f32[512,8]{0,1:T(8,128)S(1)} fusion(f32[1024,512,8]{1,0,2:T(8,128)} %get-tuple-element.32, f32[512,8]{0,1:T(8,128)S(1)} %get-tuple-element.31, pred[512,1024]{0,1:T(8,128)(4,1)S(1)} %copy-done), kind=kLoop, calls=%fused_computation.2 | loop fusion | flops 16773120 | bytes 17334272 | tf_op jit(solution)/shard_map/reduce_sum | solution.py:50
  556.5 9.1 %fusion.7 = bf16[1,128,512,8]{2,1,3,0:T(8,128)(2,1)S(1)} fusion(f32[1024,512,8]{1,0,2:T(8,128)} %get-tuple-element.32, f32[512,8]{0,1:T(8,128)S(1)} %get-tuple-element.31, pred[512,1024]{0,1:T(8,128)(4,1)S(1)} %copy-done, f32[512,8]{0,1:T(8,128)S(1)} %fusion, bf16[512,1,128]{2,0,1:T(8,128)(2,1)S(1)} %copy-done.4, bf16[512,1,128]{2,0,1:T(8,128)(2,1)S(1)} %copy-done.10), kind=kOutput, calls=%fused_computation.10 | convolution fusion | flops 1092091904 | bytes 18644992 | tf_op jit(solution)/shard_map/qkgs,skd->qkgd/dot_general | solution.py:51
  565.7 1.3 copy.29
  567.0 72.5 %psum.31 = f32[64,1,8]{0,2,1:T(8,128)S(1)} all-reduce(f32[64,1,8]{0,2,1:T(8,128)S(1)} %copy-done.8), channel_id=1, replica_groups=mesh['ctx'=32,'tp'=8] {'ctx'}, use_global_device_ids=true, to_apply=%region_9.10 | all-reduce | flops 512 | bytes 4096 | tf_op jit(solution)/shard_map/psum | solution.py:134
  639.5 41.2 %all-reduce.5.cloned.1.call-done = f32[64,1,8,128]{3,0,2,1:T(8,128)} async-done(((f32[64,1,8,128]{3,0,2,1:T(8,128)}), f32[64,1,8,128]{3,0,2,1:T(8,128)}) %all-reduce.5.cloned.1.call-update) | async-done | bytes 262160 | tf_op jit(solution)/shard_map/psum | solution.py:134
  680.7 1.3 fusion.19
  (63 shorter events, 14.3 us)
Async XLA Ops:
  7.2 57.1 %all-gather.6.cloned.1.call-start = ((), (), s32[]{:S(2)}) async-start(), calls=%async_computation | async-start | bytes 9437184 | tf_op jit(solution)/shard_map/all_gather | solution.py:73
  7.9 83.5 %all-gather.8.cloned.1.call-start = ((), (), s32[]{:S(2)}) async-start(), calls=%async_computation.1 | async-start | bytes 1179648 | tf_op jit(solution)/shard_map/all_gather | solution.py:74
  8.6 164.9 %all-gather.12.cloned.1.call-start = ((), (), s32[]{:S(2)}) async-start(), calls=%async_computation.3 | async-start | bytes 2162688 | tf_op jit(solution)/shard_map/all_gather | solution.py:85
  9.4 241.7 %all-gather.10.cloned.1.call-start = ((), (), s32[]{:S(2)}) async-start(), calls=%async_computation.2 | async-start | bytes 2162688 | tf_op jit(solution)/shard_map/all_gather | solution.py:90
  10.0 381.4 %all-gather.14.cloned.1.call-start = ((), (), s32[]{:S(2)}) async-start(), calls=%async_computation.4 | async-start | bytes 17301504 | tf_op jit(solution)/shard_map/all_gather | solution.py:80
  10.5 525.5 %all-reduce.7.cloned.1.call-start = ((), (), s32[]{:S(2)}) async-start(), calls=%async_computation.6 | async-start | bytes 524288 | tf_op jit(solution)/shard_map/psum | solution.py:12
  71.9 107.5 %copy-start.9 = (f32[64]{0:T(128)S(1)}, f32[64]{0:T(128)}, u32[]{:S(2)}) copy-start(f32[64]{0:T(128)} %constant.24.clone) | copy-start | bytes 772
  180.6 225.7 %copy-start.1 = (bf16[512,1,64]{2,0,1:T(8,128)(2,1)}, bf16[512,1,64]{2,0,1:T(8,128)(2,1)S(1)}, u32[]{:S(2)}) copy-start(bf16[512,1,64]{2,0,1:T(8,128)(2,1)S(1)} %get-tuple-element.15) | copy-start | bytes 196612
  258.0 133.4 %copy-start.2 = (bf16[576,128]{1,0:T(8,128)(2,1)}, bf16[576,128]{1,0:T(8,128)(2,1)S(1)}, u32[]{:S(2)}) copy-start(bf16[576,128]{1,0:T(8,128)(2,1)S(1)} %convolution_convert_fusion) | copy-start | bytes 442372
  258.8 421.9 %all-reduce.5.cloned.1.call-start = ((), (), s32[]{:S(2)}) async-start(), calls=%async_computation.5 | async-start | bytes 524288 | tf_op jit(solution)/shard_map/psum | solution.py:134
  480.6 2.5 copy-start.7
  480.6 3.1 copy-start.3
  536.1 10.7 %copy-start = (pred[512,1024]{0,1:T(8,128)(4,1)S(1)}, pred[512,1024]{0,1:T(8,128)(4,1)}, u32[]{:S(2)}) copy-start(pred[512,1024]{0,1:T(8,128)(4,1)} %concatenate.62) | copy-start | bytes 1572868
  546.8 9.3 %copy-start.5 = (bf16[64,64]{1,0:T(8,128)(2,1)S(1)}, bf16[64,64]{1,0:T(8,128)(2,1)}, u32[]{:S(2)}) copy-start(bf16[64,64]{1,0:T(8,128)(2,1)} %get-tuple-element.20) | copy-start | bytes 24580
  546.8 9.3 %copy-start.6 = (bf16[64,64]{1,0:T(8,128)(2,1)S(1)}, bf16[64,64]{1,0:T(8,128)(2,1)}, u32[]{:S(2)}) copy-start(bf16[64,64]{1,0:T(8,128)(2,1)} %get-tuple-element.21) | copy-start | bytes 24580
  546.8 9.6 %copy-start.4 = (bf16[512,1,128]{2,0,1:T(8,128)(2,1)S(1)}, bf16[512,1,128]{2,0,1:T(8,128)(2,1)}, u32[]{:S(2)}) copy-start(bf16[512,1,128]{2,0,1:T(8,128)(2,1)} %get-tuple-element.18) | copy-start | bytes 393220
  546.8 9.6 %copy-start.10 = (bf16[512,1,128]{2,0,1:T(8,128)(2,1)S(1)}, bf16[512,1,128]{2,0,1:T(8,128)(2,1)}, u32[]{:S(2)}) copy-start(bf16[512,1,128]{2,0,1:T(8,128)(2,1)} %get-tuple-element.7) | copy-start | bytes 393220
  556.5 10.5 %copy-start.8 = (f32[64,1,8]{0,2,1:T(8,128)S(1)}, f32[64,1,8]{0,2,1:T(8,128)}, u32[]{:S(2)}) copy-start(f32[64,1,8]{0,2,1:T(8,128)} %get-tuple-element.25) | copy-start | bytes 6148
Sparse Core Ops, SparseCore 0:
  9.8 54.4 all-gather.5
  66.1 25.2 all-gather.7
  94.0 79.4 all-gather.11
  176.0 75.1 all-gather.9
  253.6 137.7 all-gather.13
  394.7 141.2 all-reduce.6
  539.5 141.1 all-reduce.4
where the time goes:
time: 690 us
  waiting for transfers between devices  440 us (64%)
  blocking collectives  144 us (21%)
  matrix products  51.5 us (7%)
  other arithmetic  23.5 us (3%)
  local copies, waits for them, and re-layouts  15.8 us (2%)
  between operations  14.4 us (2%)
    all_gather x1, waiting for transfers between devices, on_device(): lax.all_gather(query_matrix, 'ctx', axis=0, tiled=True)  133 us
    all_gather x1, waiting for transfers between devices, on_device(): lax.all_gather(key_matrix, 'ctx', axis=0, tiled=True)  79.8 us
    psum x1, blocking collectives, on_device(): lax.psum((total * scaled, mixed * scaled[..., None]), 'ctx')  72.5 us
    pmax x1, blocking collectives, on_device(): top = lax.pmax(peak, 'ctx')  71.4 us
    all_gather x1, waiting for transfers between devices, on_device(): lax.all_gather(value_matrix, 'ctx', axis=0, tiled=True)  68.9 us
    psum x1, waiting for transfers between devices, from_root(): return lax.psum(kept, axis)  47.8 us
    all_gather x1, waiting for transfers between devices, on_device(): lax.all_gather(context_block_rows, 'tp', axis=1, tiled=True)  47.3 us
    psum x1, waiting for transfers between devices, on_device(): lax.psum((total * scaled, mixed * scaled[..., None]), 'ctx')  41.2 us
  transfers between devices with their start and end apart: 7, of which 7 were waited for; matrix products, arithmetic and copies ran while one was open for 13% of the time, Pallas kernels for 0%

commit v1 on v0

--- a/solution.py
+++ b/solution.py
@@ -5,6 +5,18 @@
 from jax.sharding import PartitionSpec as P
 
 HEAD_SIZE = 128
+
+
+def collect(x, axis, dim):
+    ways, here = (lax.axis_size(axis), lax.axis_index(axis))
+    grown, reach = (x, 1)
+    while reach < ways:
+        theirs = lax.ppermute(grown, axis, [(d, d ^ reach) for d in range(ways)])
+        mine_first = jnp.concatenate([grown, theirs], axis=dim)
+        theirs_first = jnp.concatenate([theirs, grown], axis=dim)
+        grown = jnp.where(here & reach == 0, mine_first, theirs_first)
+        reach = 2 * reach
+    return grown
 
 
 def from_root(value, axis, source):
@@ -71,7 +83,7 @@
     head_group = heads_q // heads_kv
     whole_rows, whole_query = (
         lax.all_gather(context_block_rows, "tp", axis=1, tiled=True),
-        lax.all_gather(query_hidden_rows, "tp", axis=1, tiled=True),
+        collect(query_hidden_rows, "tp", 1),
     )
     stacked = jnp.concatenate([whole_rows, whole_query], 0)
     head_rows = blk + qcount

time: 690 us -> 662 us (0.959)
  waiting for transfers between devices: 440 us -> 415 us
  local copies, waits for them, and re-layouts: 15.8 us -> 5.88 us
    all_gather x1, waiting for transfers between devices: 79.8 us -> 54.4 us  [on_device(): lax.all_gather(key_matrix, 'ctx', axis=0, tiled=True)]
    all_gather x1 -> x0, waiting for transfers between devices: 19.5 us -> none  [on_device(): lax.all_gather(query_hidden_rows, 'tp', axis=1, tiled=True)]
    ppermute x0 -> x3, waiting for transfers between devices: none -> 15.1 us  [collect(): theirs = lax.ppermute(grown, axis, [(d, d ^ reach) for d in range(ways)])]
    unnamed x29 -> x28, local copies, waits for them, and re-layouts: 10.3 us -> 2.72 us
  transfers between devices with their start and end apart: 7 -> 9, of which waited for: 7 -> 9; matrix products, arithmetic and copies ran while one was open for 13% -> 12% of each run, Pallas kernels for 0% -> 0%
where the time goes in v1:
time: 662 us
  waiting for transfers between devices  415 us (63%)
  blocking collectives  144 us (22%)
  matrix products  53.5 us (8%)
  other arithmetic  24.9 us (4%)
  between operations  14.4 us (2%)
    all_gather x1, waiting for transfers between devices, on_device(): lax.all_gather(query_matrix, 'ctx', axis=0, tiled=True)  133 us
    psum x1, blocking collectives, on_device(): lax.psum((total * scaled, mixed * scaled[..., None]), 'ctx')  72.5 us
    all_gather x1, waiting for transfers between devices, on_device(): lax.all_gather(value_matrix, 'ctx', axis=0, tiled=True)  71.5 us
    pmax x1, blocking collectives, on_device(): top = lax.pmax(peak, 'ctx')  71.2 us
    all_gather x1, waiting for transfers between devices, on_device(): lax.all_gather(key_matrix, 'ctx', axis=0, tiled=True)  54.4 us
    all_gather x1, waiting for transfers between devices, on_device(): lax.all_gather(context_block_rows, 'tp', axis=1, tiled=True)  50.5 us
    psum x1, waiting for transfers between devices, from_root(): return lax.psum(kept, axis)  47.2 us
    psum x1, waiting for transfers between devices, on_device(): lax.psum((total * scaled, mixed * scaled[..., None]), 'ctx')  41 us
  transfers between devices with their start and end apart: 9, of which 9 were waited for; matrix products, arithmetic and copies ran while one was open for 12% of the time, Pallas kernels for 0%

profile of v1, /device:TPU:2, one launch (start us, length us, event | category | flops | bytes accessed | tf_op | source)
XLA Modules:
  0.0 662.0 jit_solution(17620882640962045848)
XLA Ops:
  10.2 1.4 collective-permute-done
  12.7 2.4 collective-permute-start.1
  16.6 1.4 broadcast_compare_fusion
  18.0 3.7 collective-permute-done.1
  21.8 1.7 collective-permute-start.2
  24.3 2.5 multiply_cosine_fusion
  26.8 10.0 %collective-permute-done.2 = bf16[64,4096]{1,0:T(8,128)(2,1)S(1)} collective-permute-done((bf16[64,4096]{1,0:T(8,128)(2,1)S(1)}, bf16[64,4096]{1,0:T(8,128)(2,1)S(1)}, u32[]{:S(2)}, u32[]{:S(2)}) %collective-permute-start.2) | collective-permute-done | bytes 524320 | tf_op jit(solution)/shard_map/ppermute | solution.py:14
  37.1 54.4 %all-gather.9.cloned.1.call-done = bf16[8192,128]{1,0:T(8,128)(2,1)} async-done(((bf16[256,128]{1,0:T(8,128)(2,1)}), bf16[8192,128]{1,0:T(8,128)(2,1)}) %all-gather.9.cloned.1.call-update) | async-done | bytes 2097168 | tf_op jit(solution)/shard_map/all_gather | solution.py:97
  91.5 50.5 %all-gather.5.cloned.1.call-done = bf16[512,8192]{1,0:T(8,128)(2,1)} async-done(((bf16[512,1024]{1,0:T(8,128)(2,1)}), bf16[512,8192]{1,0:T(8,128)(2,1)}) %all-gather.5.cloned.1.call-update) | async-done | bytes 8388624 | tf_op jit(solution)/shard_map/all_gather | solution.py:85
  142.0 7.1 %fusion.8 = f32[576,128]{1,0:T(8,128)S(1)} fusion(bf16[8192,128]{1,0:T(8,128)(2,1)} %all-gather.9.cloned.1.call-done, bf16[64,8192]{1,0:T(8,128)(2,1)S(1)} %maximum_select_fusion, bf16[512,8192]{1,0:T(8,128)(2,1)} %all-gather.5.cloned.1.call-done), kind=kOutput, calls=%fused_computation.10 | convolution fusion | flops 1226833920 | bytes 11829248 | tf_op jit(solution)/shard_map/dot_general | solution.py:95
  152.0 71.5 %all-gather.7.cloned.1.call-done = bf16[8192,128]{1,0:T(8,128)(2,1)} async-done(((bf16[256,128]{1,0:T(8,128)(2,1)}), bf16[8192,128]{1,0:T(8,128)(2,1)}) %all-gather.7.cloned.1.call-update) | async-done | bytes 2097168 | tf_op jit(solution)/shard_map/all_gather | solution.py:102
  223.6 6.6 fusion.22
  231.2 132.6 %all-gather.11.cloned.1.call-done = bf16[8192,1024]{1,0:T(8,128)(2,1)} async-done(((bf16[256,1024]{1,0:T(8,128)(2,1)}), bf16[8192,1024]{1,0:T(8,128)(2,1)}) %all-gather.11.cloned.1.call-update) | async-done | bytes 16777232 | tf_op jit(solution)/shard_map/all_gather | solution.py:92
  363.8 15.8 %fusion.7 = f32[576,1024]{1,0:T(8,128)S(1)} fusion(bf16[8192,1024]{1,0:T(8,128)(2,1)} %all-gather.11.cloned.1.call-done, bf16[64,8192]{1,0:T(8,128)(2,1)S(1)} %maximum_select_fusion, bf16[512,8192]{1,0:T(8,128)(2,1)} %all-gather.5.cloned.1.call-done), kind=kOutput, calls=%fused_computation.9 | convolution fusion | flops 9682550784 | bytes 28573696 | tf_op jit(solution)/shard_map/dot_general | solution.py:90
  380.2 1.4 fusion.88
  382.5 71.2 %pmax.7 = f32[64,1,8]{0,2,1:T(8,128)S(1)} all-reduce(f32[64,1,8]{0,2,1:T(8,128)S(1)} %bitcast.166), channel_id=1, replica_groups=mesh['ctx'=32,'tp'=8] {'ctx'}, use_global_device_ids=true, to_apply=%region_5.6 | all-reduce | flops 512 | bytes 4096 | tf_op jit(solution)/shard_map/pmax | solution.py:144
  454.3 2.0 fusion.86
  457.9 3.5 subtract_convert_fusion
  461.4 47.2 %all-reduce.7.cloned.1.call-done = (bf16[512,1,128]{2,0,1:T(8,128)(2,1)}, bf16[512,1,128]{2,0,1:T(8,128)(2,1)}) async-done(((bf16[512,1,128]{2,0,1:T(8,128)(2,1)}, bf16[512,1,128]{2,0,1:T(8,128)(2,1)}), (bf16[512,1,128]{2,0,1:T(8,128)(2,1)}, bf16[512,1,128]{2,0,1:T(8,128)(2,1)})) %all-reduce.7.cloned.1.call-update) | async-done | bytes 262160 | tf_op jit(solution)/shard_map/psum | solution.py:24
  508.6 10.7 %fusion.2 = (f32[512,8]{0,1:T(8,128)S(1)}, f32[1024,512,8]{1,0,2:T(8,128)}) fusion(pred[512,1024]{0,1:T(8,128)(4,1)} %concatenate.86, bf16[512,8,64]{2,0,1:T(8,128)(2,1)} %get-tuple-element.9, bf16[512,8,64]{2,0,1:T(8,128)(2,1)S(1)} %get-tuple-element.8, bf16[512,1,64]{2,0,1:T(8,128)(2,1)} %copy-done.1, bf16[512,1,64]{2,0,1:T(8,128)(2,1)S(1)} %get-tuple-element.14, ...), kind=kOutput, calls=%fused_computation.4 | convolution fusion | flops 1089204224 | bytes 18628608 | tf_op jit(solution)/shard_map/qkgd,skd->qkgs/dot_general | solution.py:56
  519.3 9.3 %fusion = f32[512,8]{0,1:T(8,128)S(1)} fusion(f32[1024,512,8]{1,0,2:T(8,128)} %get-tuple-element.32, f32[512,8]{0,1:T(8,128)S(1)} %get-tuple-element.31, pred[512,1024]{0,1:T(8,128)(4,1)S(1)} %copy-done), kind=kLoop, calls=%fused_computation.2 | loop fusion | flops 16773120 | bytes 17334272 | tf_op jit(solution)/shard_map/reduce_sum | solution.py:62
  529.0 9.1 %fusion.10 = bf16[1,128,512,8]{2,1,3,0:T(8,128)(2,1)S(1)} fusion(f32[1024,512,8]{1,0,2:T(8,128)} %get-tuple-element.32, f32[512,8]{0,1:T(8,128)S(1)} %get-tuple-element.31, pred[512,1024]{0,1:T(8,128)(4,1)S(1)} %copy-done, f32[512,8]{0,1:T(8,128)S(1)} %fusion, bf16[512,1,128]{2,0,1:T(8,128)(2,1)S(1)} %copy-done.4, bf16[512,1,128]{2,0,1:T(8,128)(2,1)S(1)} %copy-done.10), kind=kOutput, calls=%fused_computation.14 | convolution fusion | flops 1092091904 | bytes 18644992 | tf_op jit(solution)/shard_map/qkgs,skd->qkgd/dot_general | solution.py:63
  539.5 72.5 %psum.31 = f32[64,1,8]{0,2,1:T(8,128)S(1)} all-reduce(f32[64,1,8]{0,2,1:T(8,128)S(1)} %copy-done.8), channel_id=1, replica_groups=mesh['ctx'=32,'tp'=8] {'ctx'}, use_global_device_ids=true, to_apply=%region_9.10 | all-reduce | flops 512 | bytes 4096 | tf_op jit(solution)/shard_map/psum | solution.py:146
  612.1 41.0 %all-reduce.5.cloned.1.call-done = f32[64,1,8,128]{3,0,2,1:T(8,128)} async-done(((f32[64,1,8,128]{3,0,2,1:T(8,128)}), f32[64,1,8,128]{3,0,2,1:T(8,128)}) %all-reduce.5.cloned.1.call-update) | async-done | bytes 262160 | tf_op jit(solution)/shard_map/psum | solution.py:146
  (67 shorter events, 18.0 us)
Async XLA Ops:
  7.2 84.3 %all-gather.9.cloned.1.call-start = ((), (), s32[]{:S(2)}) async-start(), calls=%async_computation.2 | async-start | bytes 2162688 | tf_op jit(solution)/shard_map/all_gather | solution.py:97
  7.9 134.1 %all-gather.5.cloned.1.call-start = ((), (), s32[]{:S(2)}) async-start(), calls=%async_computation | async-start | bytes 9437184 | tf_op jit(solution)/shard_map/all_gather | solution.py:85
  8.6 214.9 %all-gather.7.cloned.1.call-start = ((), (), s32[]{:S(2)}) async-start(), calls=%async_computation.1 | async-start | bytes 2162688 | tf_op jit(solution)/shard_map/all_gather | solution.py:102
  9.4 354.5 %all-gather.11.cloned.1.call-start = ((), (), s32[]{:S(2)}) async-start(), calls=%async_computation.3 | async-start | bytes 17301504 | tf_op jit(solution)/shard_map/all_gather | solution.py:92
  10.0 498.6 %all-reduce.7.cloned.1.call-start = ((), (), s32[]{:S(2)}) async-start(), calls=%async_computation.5 | async-start | bytes 524288 | tf_op jit(solution)/shard_map/psum | solution.py:24
  10.0 1.6 collective-permute-start
  12.7 9.0 %collective-permute-start.1 = (bf16[64,2048]{1,0:T(8,128)(2,1)S(1)}, bf16[64,2048]{1,0:T(8,128)(2,1)S(1)}, u32[]{:S(2)}, u32[]{:S(2)}) collective-permute-start(bf16[64,2048]{1,0:T(8,128)(2,1)S(1)} %maximum_select_fusion.2), channel_id=1, source_target_pairs={{0,2},{1,3},{2,0},{3,1},{4,6},{5,7},{6,4},{7,5},{8,10},{9,11},{10,... | collective-permute-start | bytes 786440 | tf_op jit(solution)/shard_map/ppermute | solution.py:14
  21.8 15.1 %collective-permute-start.2 = (bf16[64,4096]{1,0:T(8,128)(2,1)S(1)}, bf16[64,4096]{1,0:T(8,128)(2,1)S(1)}, u32[]{:S(2)}, u32[]{:S(2)}) collective-permute-start(bf16[64,4096]{1,0:T(8,128)(2,1)S(1)} %maximum_select_fusion.1), channel_id=1, source_target_pairs={{0,4},{1,5},{2,6},{3,7},{4,0},{5,1},{6,2},{7,3},{8,12},{9,13},{10,... | collective-permute-start | bytes 1572872 | tf_op jit(solution)/shard_map/ppermute | solution.py:14
  37.1 112.1 %copy-start.9 = (f32[64]{0:T(128)S(1)}, f32[64]{0:T(128)}, u32[]{:S(2)}) copy-start(f32[64]{0:T(128)} %constant.33.clone) | copy-start | bytes 772
  150.4 79.7 %copy-start.1 = (bf16[512,1,64]{2,0,1:T(8,128)(2,1)}, bf16[512,1,64]{2,0,1:T(8,128)(2,1)S(1)}, u32[]{:S(2)}) copy-start(bf16[512,1,64]{2,0,1:T(8,128)(2,1)S(1)} %get-tuple-element.15) | copy-start | bytes 196612
  230.2 149.5 %copy-start.2 = (bf16[576,128]{1,0:T(8,128)(2,1)}, bf16[576,128]{1,0:T(8,128)(2,1)S(1)}, u32[]{:S(2)}) copy-start(bf16[576,128]{1,0:T(8,128)(2,1)S(1)} %fusion.22) | copy-start | bytes 442372
  231.0 422.1 %all-reduce.5.cloned.1.call-start = ((), (), s32[]{:S(2)}) async-start(), calls=%async_computation.4 | async-start | bytes 524288 | tf_op jit(solution)/shard_map/psum | solution.py:146
  453.8 2.5 copy-start.7
  453.8 3.1 copy-start.3
  508.6 10.7 %copy-start = (pred[512,1024]{0,1:T(8,128)(4,1)S(1)}, pred[512,1024]{0,1:T(8,128)(4,1)}, u32[]{:S(2)}) copy-start(pred[512,1024]{0,1:T(8,128)(4,1)} %concatenate.86) | copy-start | bytes 1572868
  519.3 9.3 %copy-start.5 = (bf16[64,64]{1,0:T(8,128)(2,1)S(1)}, bf16[64,64]{1,0:T(8,128)(2,1)}, u32[]{:S(2)}) copy-start(bf16[64,64]{1,0:T(8,128)(2,1)} %get-tuple-element.20) | copy-start | bytes 24580
  519.3 9.3 %copy-start.6 = (bf16[64,64]{1,0:T(8,128)(2,1)S(1)}, bf16[64,64]{1,0:T(8,128)(2,1)}, u32[]{:S(2)}) copy-start(bf16[64,64]{1,0:T(8,128)(2,1)} %get-tuple-element.21) | copy-start | bytes 24580
  519.3 9.6 %copy-start.4 = (bf16[512,1,128]{2,0,1:T(8,128)(2,1)S(1)}, bf16[512,1,128]{2,0,1:T(8,128)(2,1)}, u32[]{:S(2)}) copy-start(bf16[512,1,128]{2,0,1:T(8,128)(2,1)} %get-tuple-element.18) | copy-start | bytes 393220
  519.3 9.6 %copy-start.10 = (bf16[512,1,128]{2,0,1:T(8,128)(2,1)S(1)}, bf16[512,1,128]{2,0,1:T(8,128)(2,1)}, u32[]{:S(2)}) copy-start(bf16[512,1,128]{2,0,1:T(8,128)(2,1)} %get-tuple-element.7) | copy-start | bytes 393220
  529.0 10.6 %copy-start.8 = (f32[64,1,8]{0,2,1:T(8,128)S(1)}, f32[64,1,8]{0,2,1:T(8,128)}, u32[]{:S(2)}) copy-start(f32[64,1,8]{0,2,1:T(8,128)} %get-tuple-element.25) | copy-start | bytes 6148
Sparse Core Ops, SparseCore 0:
  10.6 80.8 all-gather.8
  93.3 48.6 all-gather.4
  144.6 78.9 all-gather.6
  226.0 137.7 all-gather.10
  367.2 141.3 all-reduce.6
  511.9 141.1 all-reduce.4
